TPU v7x, 512 devices: a whole 4x4x16 slice. The times are simulated.
512 devices in a mesh: scen: 64 (over z, y), section: 8 (over x, core).
Axes of the slice: x: 4, y: 4, z: 16, core: 2. Of those that a mesh axis runs over, the one named last changes fastest.
Arguments:
- scen_inverse: bfloat16 [1536, 512, 512], P(('scen', 'section')), as said below
- link_border: bfloat16 [1536, 512, 896], P(('scen', 'section'))
- scen_rhs: bfloat16 [1536, 512], P(('scen', 'section')), may hold values from -0.59765625 to 0.59765625
- link_mask: int32 [1536, 7], P(('scen', 'section')), may hold values 0 or 1
- live_slots: int32 [512], P(('scen', 'section')), may hold values from 1 to 3, as said below
- first_block: float32 [896, 896], P('scen', 'section'), as said below
- first_rhs: float32 [896], replicated, may hold values from -120 to 120
Outputs:
- first_step: float32 [896], replicated
- scen_step: float32 [1536, 512], P(('scen', 'section'))
Inputs may be any that keep to these rules, and one draw needn't show every extreme that they name: The first live_slots[d] of device d's 3 slots hold scenarios; some device has all 3 slots live. `scen_inverse`: each scen_inverse_s is symmetric and positive definite. first_block is symmetric with a dominant positive diagonal.
All inputs are finite; a program needn't handle non-finite values. No bound on the sum of `link_mask` on one device may be relied on, other than what follows from the above.
Results may differ from a plain program's by a relative error of at most 0.0024.
Values sent between devices are 32-bit elements; how exact they have to be, the bound alone decides.
No kernel may reach another device: no remote copies, remote signals or barrier semaphores. Data moves between devices by JAX's collectives and lax.ppermute only.
A program may use at most 64 MiB of HBM per device.

v0:
```python
import functools

import jax
import jax.numpy as jnp
from jax import lax
from jax.experimental import pallas as pl
from jax.experimental.pallas import tpu as pltpu
from jax.sharding import PartitionSpec as P

SIDE = 4
STRIP = 4
LANES = 128
SUBLANES = 8
F32 = jnp.float32
BF16 = jnp.bfloat16
ROWS_ALONE = (((1,), (1,)), ((), ()))


def halves(value):
    high = value.astype(BF16)
    return high, (value - high.astype(F32)).astype(BF16)


def dot(left, right):
    return jnp.dot(left, right, preferred_element_type=F32)


def dot_rows(left, right):
    return lax.dot_general(left, right, ROWS_ALONE, preferred_element_type=F32)


def mixed(left, right):
    left_high, left_low = halves(left)
    right_high, right_low = halves(right)
    return dot(
        jnp.concatenate([left_high, left_low, left_high], axis=1),
        jnp.concatenate([right_high, right_high, right_low], axis=0),
    )


def mixed_rows(left, right):
    left_high, left_low = halves(left)
    right_high, right_low = halves(right)
    return dot_rows(
        jnp.concatenate([left_high, left_low, left_high], axis=1),
        jnp.concatenate([right_high, right_high, right_low], axis=1),
    )


def panel_base(j, blocks):
    return LANES * (j * blocks - j * (j - 1) // 2)


def terms_kernel(
    blocks, live_ref, place_ref, mask_hbm, inverse_hbm, border_ref, right_hbm, corner_hbm, first_ref,
    keep_ref, send_ref, product_ref, reduced_ref, total_ref, rows_ref, corner_wide_ref, rhs_ref,
    mask_ref, inverse_ref, right_ref, corner_ref, small_sems, inverse_sems,
):
    slot = pl.program_id(0)
    width = blocks * LANES
    corner_rows, corner_cols = corner_ref.shape
    small = [
        pltpu.make_async_copy(source, target, small_sems.at[i])
        for i, (source, target) in enumerate(
            ((mask_hbm, mask_ref), (right_hbm, right_ref), (corner_hbm, corner_ref))
        )
    ]

    def fetch(at):
        return pltpu.make_async_copy(inverse_hbm.at[at], inverse_ref.at[at], inverse_sems.at[at])

    @pl.when(slot == 0)
    def start():
        for at in range(inverse_ref.shape[0]):
            fetch(at).start()
        for copy in small:
            copy.start()
        total_ref[...] = jnp.zeros_like(total_ref)
        corner_wide_ref[...] = jnp.zeros_like(corner_wide_ref)
        for copy in small:
            copy.wait()
        corner_wide_ref[0:corner_rows, 0:corner_cols] = corner_ref[...]
        row_start = place_ref[0] * corner_rows
        col_start = place_ref[1] * corner_cols
        row_base = row_start // SUBLANES * SUBLANES
        col_base = col_start // LANES * LANES
        moved = pltpu.roll(corner_wide_ref[...], col_start - col_base, 1)
        moved = pltpu.roll(moved, row_start - row_base, 0)
        total_ref[
            pl.ds(pl.multiple_of(row_base, SUBLANES), corner_wide_ref.shape[0]),
            pl.ds(pl.multiple_of(col_base, LANES), corner_wide_ref.shape[1]),
        ] = moved
        at_origin = jnp.logical_and(place_ref[0] == 0, place_ref[1] == 0)
        rhs_ref[...] = jnp.where(at_origin, first_ref[...], 0.0)

    fetch(slot).wait()

    @pl.when(slot < live_ref[0])
    def add():
        mask = mask_ref[...]
        mask = jnp.sum(jnp.where(lax.broadcasted_iota(jnp.int32, mask.shape, 0) == slot, mask, 0), axis=0, keepdims=True)
        for c in range(blocks):
            at = slice(c * LANES, (c + 1) * LANES)
            turned = border_ref[0, :, at].T
            rows_ref[at, :] = turned * mask[:, c : c + 1].astype(F32).astype(BF16)
        inverse = inverse_ref[slot]
        product = dot(rows_ref[...], inverse).astype(BF16)
        product_ref[0] = product
        right = right_ref[...].astype(F32)
        right = jnp.sum(jnp.where(lax.broadcasted_iota(jnp.int32, right.shape, 0) == slot, right, 0.0), axis=0, keepdims=True)
        right = jnp.broadcast_to(right, (16, right.shape[1])).astype(BF16)
        reduced = dot(right, inverse)[0:1]
        reduced_ref[0] = reduced
        first, rest = halves(reduced)
        rest_wide = reduced - first.astype(F32)
        second, third = halves(rest_wide)
        row = lax.broadcasted_iota(jnp.int32, (16, reduced.shape[1]), 0)
        pieces = jnp.where(
            row == 0, first.astype(F32), jnp.where(row == 1, second.astype(F32), jnp.where(row == 2, third.astype(F32), 0.0))
        ).astype(BF16)
        rhs_ref[...] += jnp.sum(dot_rows(pieces, rows_ref[...]), axis=0, keepdims=True)
        for c in range(0, width, 2 * LANES):
            end = min(c + 2 * LANES, width)
            total_ref[c:width, c:end] += dot_rows(rows_ref[c:width, :], product[c:end, :])

    @pl.when(slot == pl.num_programs(0) - 1)
    def finish():
        cut = LANES // 2
        right_half = lax.broadcasted_iota(jnp.int32, (1, LANES), 1) >= cut
        places = [(j, i) for j in range(blocks) for i in range(j, blocks)]
        count = len(places) // 2

        def write(out_ref, own_places):
            for at, (j, i) in enumerate(own_places):
                base = at * LANES
                out_ref[base : base + LANES, :] = total_ref[i * LANES : (i + 1) * LANES, j * LANES : (j + 1) * LANES]
                if i == j:
                    own = rhs_ref[:, j * LANES : (j + 1) * LANES]
                    for row, value in ((0, own), (cut - 1, pltpu.roll(own, cut, 1))):
                        line = slice(base + row, base + row + 1)
                        out_ref[line, :] = jnp.where(right_half, value, out_ref[line, :])

        for core in range(2):

            @pl.when(lax.rem(place_ref[1], 2) == core)
            def write_both():
                write(keep_ref, places[core * count : (core + 1) * count])
                write(send_ref, places[(1 - core) * count : (2 - core) * count])


def invert(rows):
    count = len(rows)
    shape = (SUBLANES, LANES)
    lane = lax.broadcasted_iota(jnp.int32, shape, 1)
    sublane = lax.broadcasted_iota(jnp.int32, shape, 0)

    def across(block, c):
        return jnp.broadcast_to(block[:, c : c + 1], shape)

    def down(block, k):
        return jnp.broadcast_to(block[k : k + 1, :], shape)

    for p in range(count):
        at = p * SUBLANES
        strip = range(p // STRIP * STRIP, (p // STRIP + 1) * STRIP)
        carried = p + 1 in strip
        if p == strip[0]:
            own_columns = [across(rows[p], at + k) for k in range(SUBLANES)]
        inside = jnp.logical_and(lane >= at, lane < at + SUBLANES)
        own = jnp.where(inside, jnp.where(lane - at == sublane, 1.0, 0.0), rows[p])
        columns = [own_columns]
        following = []
        if carried:
            following = [across(rows[p + 1], at + k) for k in range(SUBLANES)]
            columns[0] = columns[0] + [across(rows[p], at + SUBLANES + k) for k in range(SUBLANES)]
            columns.append(following + [across(rows[p + 1], at + SUBLANES + k) for k in range(SUBLANES)])
        same = jnp.zeros(shape, F32)
        cross = jnp.zeros(shape, F32)
        for k in range(0, SUBLANES, 2):
            one, two = columns[0][k], columns[0][k + 1]
            a, b, c = down(one, k), down(two, k), down(two, k + 1)
            det = a * c - b * b
            rough = pl.reciprocal(det, approx=True)
            mend = 2.0 - det * rough
            free = jnp.logical_or(sublane < k, sublane > k + 1)
            factors = []
            for half, group in enumerate(columns):
                u, v = group[k], group[k + 1]
                first, second = ((u * c - v * b) * rough) * mend, ((v * a - u * b) * rough) * mend
                if half == 0:
                    first, second = jnp.where(free, first, 0.0), jnp.where(free, second, 0.0)
                factors.append((first, second))
            for m in range(k + 2, len(columns[0])):
                top, bottom = down(columns[0][m], k), down(columns[0][m], k + 1)
                for group, (first, second) in zip(columns, factors):
                    group[m] = (group[m] - first * top) - second * bottom
            first, second = factors[0]
            own = (own - first * down(own, k)) - second * down(own, k + 1)
            inverse = rough * mend
            same = jnp.where(sublane == k, c * inverse, jnp.where(sublane == k + 1, a * inverse, same))
            cross = jnp.where(free, cross, b * inverse)
        above, below = pltpu.roll(own, 1, 0), pltpu.roll(own, SUBLANES - 1, 0)
        own = same * own - cross * jnp.where(lax.rem(sublane, 2) == 0, below, above)
        spread = [down(own, k) for k in range(SUBLANES)]
        for v in [*range(p + 1, strip[-1] + 1), *range(strip[0], p)]:
            block = rows[v]
            spans = following if v == p + 1 else [across(block, at + k) for k in range(SUBLANES)]
            terms = [spans[k] * spread[k] for k in range(SUBLANES)]
            while len(terms) > 1:
                terms = [x + y for x, y in zip(terms[0::2], terms[1::2])]
            rows[v] = jnp.where(inside, 0.0, block) - terms[0]
        rows[p] = own
        if carried:
            own_columns = columns[1][SUBLANES:]
            continue
        others = [v % count for v in range(p + 1, p + 1 + count - STRIP)]
        rest = jnp.concatenate([rows[v] for v in others], axis=0)
        lane_wide = lax.broadcasted_iota(jnp.int32, rest.shape, 1)
        inside = jnp.logical_and(lane_wide >= strip[0] * SUBLANES, lane_wide < (p + 1) * SUBLANES)
        blank = jnp.zeros(shape, F32)
        own_rows = jnp.concatenate([rows[v] if v in strip else blank for v in range(count)], axis=0)
        rest = jnp.where(inside, 0.0, rest) - mixed(jnp.where(inside, rest, 0.0), own_rows)
        for i, v in enumerate(others):
            rows[v] = rest[i * SUBLANES : (i + 1) * SUBLANES]
    return rows


def add_up(parts):
    total = parts[0]
    for i in range(1, parts.shape[0]):
        total = total + parts[i]
    return total


def scatter_sum(value, axis, groups):
    size = len(groups[0])
    parts = value.reshape(size, value.shape[0] // size, LANES)
    return add_up(lax.all_to_all(parts, axis, 0, 0, axis_index_groups=groups))


def exchange(value, axis, groups):
    parts = jnp.broadcast_to(value[None], (len(groups[0]),) + value.shape)
    return lax.all_to_all(parts, axis, 0, 0, axis_index_groups=groups)


def gather(value, axis, groups):
    return exchange(value, axis, groups).reshape(len(groups[0]) * value.shape[0], LANES)


def sum_over_devices(keep, send):
    scen, section = lax.axis_size("scen"), lax.axis_size("section")
    depth = scen // SIDE
    far = depth // SIDE
    both = ("scen", "section")

    def at(z, y, x, core):
        return (z * SIDE + y) * section + 2 * x + core

    cores = [[2 * i, 2 * i + 1] for i in range(SIDE)]
    side = range(SIDE)
    xs, ys = (
        [[[at(z, i, k, core) if along_y else at(z, k, i, core) for i in side] for z in range(depth) for k in side]
        for core in range(2)]
        for along_y in (False, True)
    )
    first, second = xs[0] + ys[1], ys[0] + xs[1]
    near_zs = [[(z * SIDE + i) * SIDE + y for i in side] for z in range(far) for y in side]
    far_zs = [[(i * SIDE + z) * SIDE + y for i in range(far)] for z in side for y in side]
    value = keep + lax.ppermute(send, "section", [(i, i ^ 1) for i in range(section)])
    value = scatter_sum(value, both, first)
    value = scatter_sum(value, both, second)
    value = scatter_sum(value, "scen", near_zs)
    value = add_up(exchange(value, "scen", far_zs))
    value = gather(value, "scen", near_zs)
    value = gather(value, both, second)
    value = gather(value, both, first)
    return gather(value, "section", cores)


def solve_kernel(blocks, packed_ref, step_ref, work_ref, inverse_ref, turned_ref, rhs_ref, z_ref, x_ref):
    row = lax.broadcasted_iota(jnp.int32, (LANES, LANES), 0)
    column = lax.broadcasted_iota(jnp.int32, (LANES, LANES), 1)
    half = LANES // 2
    left_half = lax.broadcasted_iota(jnp.int32, (1, LANES), 1) < half
    scales, scale_columns = [], []
    for j in range(blocks):
        base = panel_base(j, blocks)
        square = packed_ref[base : base + LANES, :]
        scale = lax.rsqrt(jnp.sum(jnp.where(row == column, square, 0.0), axis=0, keepdims=True))
        scales.append(scale)
        scale_columns.append(jnp.sum(jnp.where(row == column, scale, 0.0), axis=1, keepdims=True))
        moved = pltpu.roll(square[half - 1 : half, :], half, 1)
        own = jnp.where(left_half, moved, square[0:1, :]) * scale
        rhs_ref[j] = jnp.broadcast_to(own, (SUBLANES, LANES))
    for j in range(blocks):
        for i in range(j, blocks):
            base = panel_base(j, blocks) + (i - j) * LANES
            square = packed_ref[base : base + LANES, :] * scale_columns[i] * scales[j]
            if i == j:
                square = jnp.where(row >= column, square, square.T)
            work_ref[base : base + LANES, :] = square

    def step(j, carry):
        base = pl.multiple_of(LANES * (j * blocks - lax.div(j * (j - 1), 2)), LANES)
        square = work_ref[pl.ds(base, LANES), :]
        rows = invert([square[v * SUBLANES : (v + 1) * SUBLANES] for v in range(LANES // SUBLANES)])
        inverse_ref[...] = jnp.concatenate(rows, axis=0)
        for jj in range(blocks):

            @pl.when(j == jj)
            def update():
                inverse = inverse_ref[...]
                at = panel_base(jj, blocks)
                rest = blocks - 1 - jj
                z = mixed(rhs_ref[jj], inverse)
                z_ref[jj] = z
                if rest == 0:
                    return
                panel = work_ref[at + LANES : at + (rest + 1) * LANES, :]
                turned = mixed(panel, inverse)
                turned_ref[at + LANES : at + (rest + 1) * LANES, :] = turned
                for s in range(rest):
                    left = jnp.concatenate([turned[s * LANES :, :], z], axis=0)
                    change = mixed_rows(left, panel[s * LANES : (s + 1) * LANES, :])
                    height = (rest - s) * LANES
                    target = panel_base(jj + 1 + s, blocks)
                    work_ref[target : target + height, :] -= change[:height]
                    rhs_ref[jj + 1 + s] -= change[height:]

        return carry

    lax.fori_loop(0, blocks, step, 0)
    for j in reversed(range(blocks)):
        at = panel_base(j, blocks)
        rest = blocks - 1 - j
        x = z_ref[j]
        if rest:
            x = x - mixed(x_ref[:, (j + 1) * LANES :], turned_ref[at + LANES : at + (rest + 1) * LANES, :])
        x_ref[:, j * LANES : (j + 1) * LANES] = x
    for j in range(blocks):
        at = slice(j * LANES, (j + 1) * LANES)
        step_ref[:, at] = x_ref[:, at] * scales[j]


def first_solve(packed):
    blocks = 0
    while panel_base(blocks, blocks) < packed.shape[0]:
        blocks += 1
    square = (LANES, LANES)
    return pl.pallas_call(
        functools.partial(solve_kernel, blocks),
        out_shape=jax.ShapeDtypeStruct((SUBLANES, blocks * LANES), F32),
        scratch_shapes=[
            pltpu.VMEM((packed.shape[0], LANES), F32),
            pltpu.VMEM(square, F32),
            pltpu.VMEM((packed.shape[0], LANES), F32),
            pltpu.VMEM((blocks, SUBLANES, LANES), F32),
            pltpu.VMEM((blocks, SUBLANES, LANES), F32),
            pltpu.VMEM((SUBLANES, blocks * LANES), F32),
        ],
        compiler_params=pltpu.CompilerParams(vmem_limit_bytes=48 * 1024 * 1024),
        name="first_solve",
    )(packed)


def finish_kernel(live_ref, step_ref, product_ref, reduced_ref, out_ref):
    slot = pl.program_id(0)
    first = step_ref[0:1, :]
    high, rest = halves(first)
    middle, low = halves(first - high.astype(F32))
    row = lax.broadcasted_iota(jnp.int32, (16, first.shape[1]), 0)
    pieces = jnp.where(
        row == 0, high.astype(F32), jnp.where(row == 1, middle.astype(F32), jnp.where(row == 2, low.astype(F32), 0.0))
    ).astype(BF16)
    moved = jnp.sum(dot(pieces, product_ref[0]), axis=0, keepdims=True)
    out_ref[0] = jnp.where(slot < live_ref[0], reduced_ref[0] - moved, 0.0)


def local(scen_inverse, link_border, scen_rhs, link_mask, live_slots, first_block, first_rhs):
    capacity, scen_width, link_width = link_border.shape
    blocks = link_width // LANES
    packed_rows = panel_base(blocks, blocks)
    place = jnp.stack([lax.axis_index("scen"), lax.axis_index("section")]).astype(jnp.int32)
    smem = pl.BlockSpec(memory_space=pltpu.SMEM)
    hbm = pl.BlockSpec(memory_space=pltpu.HBM)

    def in_hbm(value):
        return pltpu.with_memory_space_constraint(value, pltpu.HBM)

    def per_slot(*dims):
        return pl.BlockSpec((1,) + dims, lambda s: (s,) + (0,) * len(dims))

    def whole(*dims):
        return pl.BlockSpec(dims, lambda s: (0,) * len(dims))

    corner_height = -(-(first_block.shape[0] + SUBLANES - 1) // SUBLANES) * SUBLANES
    keep, send, product, reduced = pl.pallas_call(
        functools.partial(terms_kernel, blocks),
        grid=(capacity,),
        in_specs=[
            smem, smem, hbm, hbm,
            per_slot(scen_width, link_width),
            hbm, hbm,
            whole(1, link_width),
        ],
        out_specs=[
            whole(packed_rows // 2, LANES),
            whole(packed_rows // 2, LANES),
            per_slot(link_width, scen_width),
            per_slot(1, scen_width),
        ],
        out_shape=[
            jax.ShapeDtypeStruct((packed_rows // 2, LANES), F32),
            jax.ShapeDtypeStruct((packed_rows // 2, LANES), F32),
            jax.ShapeDtypeStruct((capacity, link_width, scen_width), BF16),
            jax.ShapeDtypeStruct((capacity, 1, scen_width), F32),
        ],
        scratch_shapes=[
            pltpu.VMEM((link_width + 2 * SUBLANES, link_width + LANES), F32),
            pltpu.VMEM((link_width, scen_width), BF16),
            pltpu.VMEM((corner_height, 2 * LANES), F32),
            pltpu.VMEM((1, link_width), F32),
            pltpu.VMEM(link_mask.shape, jnp.int32),
            pltpu.VMEM(scen_inverse.shape, BF16),
            pltpu.VMEM(scen_rhs.shape, BF16),
            pltpu.VMEM(first_block.shape, F32),
            pltpu.SemaphoreType.DMA((3,)),
            pltpu.SemaphoreType.DMA((capacity,)),
        ],
        compiler_params=pltpu.CompilerParams(vmem_limit_bytes=48 * 1024 * 1024),
        name="schur_terms",
    )(
        live_slots, place, in_hbm(link_mask), in_hbm(scen_inverse), link_border, in_hbm(scen_rhs), in_hbm(first_block),
        first_rhs[None, :],
    )
    packed = sum_over_devices(keep, send)
    step = first_solve(packed)
    scen_step = pl.pallas_call(
        finish_kernel,
        grid=(capacity,),
        in_specs=[smem, whole(SUBLANES, link_width), per_slot(link_width, scen_width), per_slot(1, scen_width)],
        out_specs=per_slot(1, scen_width),
        out_shape=jax.ShapeDtypeStruct((capacity, 1, scen_width), F32),
        compiler_params=pltpu.CompilerParams(vmem_limit_bytes=48 * 1024 * 1024),
        name="scen_steps",
    )(live_slots, step, product, reduced)
    return step[0], scen_step[:, 0, :]


def solution(mesh):
    return jax.shard_map(
        local,
        mesh=mesh,
        in_specs=(
            P(("scen", "section"), None, None),
            P(("scen", "section"), None, None),
            P(("scen", "section"), None),
            P(("scen", "section"), None),
            P(("scen", "section")),
            P("scen", "section"),
            P(),
        ),
        out_specs=(P(), P(("scen", "section"), None)),
        check_vma=False,
    )
```

profile of v0, /device:TPU:1, one launch (start us, length us, event | category | flops | bytes accessed | tf_op | source)
XLA Modules:
  0.0 144.1 jit_solution(10735231991659546009)
XLA Ops:
  1.3 0.7 broadcast_in_dim.40.first_ref
  2.0 0.1 pad_add_fusion.place_ref
  2.0 7.9 %schur_terms.1 = (f32[1792,128]{1,0:T(8,128)S(1)}, f32[1792,128]{1,0:T(8,128)S(1)}, bf16[3,896,512]{2,1,0:T(8,128)(2,1)S(1)}, f32[3,1,512]{2,1,0:T(1,128)S(1)}) custom-call(s32[1]{0:T(128)S(6)} %copy.12.live_ref, s32[2]{0:T(128)S(1)} %pad_add_fusion.place_ref, s32[3,7]{1,0:T(4,128)} %mask_hbm.1, bf16[3,512,512]{2,1,0:T(8,128)(2,1)} %inverse_hbm.1, ...), custom_call_target="tpu_custom_call" | custom-call | tf_op jit(solution)/shard_map/schur_terms/pallas_call | solution.py:397
  9.9 6.6 %collective-permute-start = (f32[1792,128]{1,0:T(8,128)S(1)}, f32[1792,128]{1,0:T(8,128)S(1)}, u32[]{:S(2)}, u32[]{:S(2)}) collective-permute-start(f32[1792,128]{1,0:T(8,128)S(1)} %get-tuple-element.7), channel_id=1, source_target_pairs={{0,1},{1,0},{2,3},{3,2},{4,5},{5,4},{6,7},{7,6},{8,9},{9,8},{10,11... | collective-permute-start | bytes 2752520 | tf_op jit(solution)/shard_map/ppermute | solution.py:269
  16.5 2.1 %collective-permute-done = f32[1792,128]{1,0:T(8,128)S(1)} collective-permute-done((f32[1792,128]{1,0:T(8,128)S(1)}, f32[1792,128]{1,0:T(8,128)S(1)}, u32[]{:S(2)}, u32[]{:S(2)}) %collective-permute-start) | collective-permute-done | bytes 917536 | tf_op jit(solution)/shard_map/ppermute | solution.py:269
  18.6 0.1 add.61
  18.7 11.8 %all_to_all.40 = f32[4,448,128]{2,1,0:T(8,128)S(1)} all-to-all(f32[4,448,128]{2,1,0:T(8,128)S(1)} %bitcast.15), channel_id=1, replica_groups={{0,2,4,6},{8,10,12,14},{16,18,20,22},{24,26,28,30},{32,34,36,38},{40,42..., dimensions={0} | all-to-all | bytes 1835008 | tf_op jit(solution)/shard_map/all_to_all | solution.py:238
  30.5 7.7 %all_to_all.41 = f32[4,112,128]{2,1,0:T(8,128)S(1)} all-to-all(f32[4,112,128]{2,1,0:T(8,128)S(1)} %bitcast.17), channel_id=1, replica_groups={{0,8,16,24},{2,10,18,26},{4,12,20,28},{6,14,22,30},{32,40,48,56},{34,42..., dimensions={0} | all-to-all | bytes 458752 | tf_op jit(solution)/shard_map/all_to_all | solution.py:238
  38.2 9.1 %all_to_all.42 = f32[4,28,128]{2,1,0:T(8,128)S(1)} all-to-all(f32[4,28,128]{2,1,0:T(8,128)S(1)} %add.69), channel_id=1, replica_groups={{0,32,64,96},{8,40,72,104},{16,48,80,112},{24,56,88,120},{128,160,192,2..., dimensions={0} | all-to-all | bytes 114688 | tf_op jit(solution)/shard_map/all_to_all | solution.py:238
  47.3 23.5 %all_to_all.43 = f32[4,28,128]{2,1,0:T(8,128)S(1)} all-to-all(f32[4,28,128]{2,1,0:T(8,128)S(1)} %broadcast_in_dim.42), channel_id=1, replica_groups={{0,128,256,384},{8,136,264,392},{16,144,272,400},{24,152,280,408},{32,1..., dimensions={0} | all-to-all | bytes 114688 | tf_op jit(solution)/shard_map/all_to_all | solution.py:243
  70.8 7.0 %all_to_all.44 = f32[4,28,128]{2,1,0:T(8,128)S(1)} all-to-all(f32[4,28,128]{2,1,0:T(8,128)S(1)} %broadcast_in_dim.44), channel_id=1, replica_groups={{0,32,64,96},{8,40,72,104},{16,48,80,112},{24,56,88,120},{128,160,192,2..., dimensions={0} | all-to-all | bytes 114688 | tf_op jit(solution)/shard_map/all_to_all | solution.py:243
  77.8 7.7 %all_to_all.45 = f32[4,112,128]{2,1,0:T(8,128)S(1)} all-to-all(f32[4,112,128]{2,1,0:T(8,128)S(1)} %broadcast_in_dim.46), channel_id=1, replica_groups={{0,8,16,24},{2,10,18,26},{4,12,20,28},{6,14,22,30},{32,40,48,56},{34,42..., dimensions={0} | all-to-all | bytes 458752 | tf_op jit(solution)/shard_map/all_to_all | solution.py:243
  85.6 0.1 broadcast_in_dim.48
  85.6 12.7 %all_to_all.46 = f32[4,448,128]{2,1,0:T(8,128)S(1)} all-to-all(f32[4,448,128]{2,1,0:T(8,128)S(1)} %broadcast_in_dim.48), channel_id=1, replica_groups={{0,2,4,6},{8,10,12,14},{16,18,20,22},{24,26,28,30},{32,34,36,38},{40,42..., dimensions={0} | all-to-all | bytes 1835008 | tf_op jit(solution)/shard_map/all_to_all | solution.py:243
  98.3 0.1 broadcast_in_dim.50
  98.4 14.7 %all_to_all.47 = f32[2,1792,128]{2,1,0:T(8,128)S(1)} all-to-all(f32[2,1792,128]{2,1,0:T(8,128)S(1)} %broadcast_in_dim.50), channel_id=1, replica_groups={{0,1},{2,3},{4,5},{6,7},{8,9},{10,11},{12,13},{14,15},{16,17},{18,19},{..., dimensions={0} | all-to-all | bytes 3670016 | tf_op jit(solution)/shard_map/all_to_all | solution.py:243
  113.1 29.0 %first_solve.1.step_ref = f32[8,896]{1,0:T(8,128)S(1)} custom-call(f32[3584,128]{1,0:T(8,128)S(1)} %bitcast.14), custom_call_target="tpu_custom_call" | custom-call | tf_op jit(solution)/shard_map/first_solve/pallas_call | solution.py:350
  142.1 0.6 slice_reduce_fusion
  142.7 0.8 scen_steps.1
  143.5 0.6 copy.11
  (9 shorter events, 0.1 us)
Async XLA Ops:
  9.9 8.7 %collective-permute-start = (f32[1792,128]{1,0:T(8,128)S(1)}, f32[1792,128]{1,0:T(8,128)S(1)}, u32[]{:S(2)}, u32[]{:S(2)}) collective-permute-start(f32[1792,128]{1,0:T(8,128)S(1)} %get-tuple-element.7), channel_id=1, source_target_pairs={{0,1},{1,0},{2,3},{3,2},{4,5},{5,4},{6,7},{7,6},{8,9},{9,8},{10,11... | collective-permute-start | bytes 2752520 | tf_op jit(solution)/shard_map/ppermute | solution.py:269
where the time goes:
time: 145 us; the launch traced here: 144 us
  blocking collectives  94.1 us (65%)
  Pallas kernels  37.6 us (26%)
  starting transfers between devices  6.6 us (5%)
  local copies, waits for them, and re-layouts  2.14 us (1%)
  waiting for transfers between devices  2.08 us (1%)
    all_to_all x5, blocking collectives, exchange(): return lax.all_to_all(parts, axis, 0, 0, axis_index_groups=groups)  65.6 us
    pallas_call x1, Pallas kernels, first_solve(): pl.pallas_call(functools.partial(solve_kernel, blocks), out_shape=jax.Sha...  29 us
    all_to_all x3, blocking collectives, scatter_sum(): return add_up(lax.all_to_all(parts, axis, 0, 0, axis_index_groups=groups))  28.5 us
    pallas_call x1, Pallas kernels, local(): pl.pallas_call(functools.partial(terms_kernel, blocks), grid=(capacity,),...  7.85 us
    ppermute x1, starting transfers between devices, sum_over_devices(): lax.ppermute(send, 'section', [(i, i ^ 1) for i in range(section)])  6.6 us
  transfers between devices with their start and end apart: 1, of which 1 were waited for; matrix products, arithmetic and copies ran while one was open for 0% of the time, Pallas kernels for 0%

commit v1 on v0

--- a/solution.py
+++ b/solution.py
@@ -257,21 +257,26 @@
         return (z * SIDE + y) * section + 2 * x + core
 
     cores = [[2 * i, 2 * i + 1] for i in range(SIDE)]
-    side = range(SIDE)
-    xs, ys = (
-        [[[at(z, i, k, core) if along_y else at(z, k, i, core) for i in side] for z in range(depth) for k in side]
-        for core in range(2)]
-        for along_y in (False, True)
-    )
-    first, second = xs[0] + ys[1], ys[0] + xs[1]
-    near_zs = [[(z * SIDE + i) * SIDE + y for i in side] for z in range(far) for y in side]
+    side, pair = range(SIDE), range(2)
+    first, second = [], []
+    for core in range(2):
+
+        def along(z, major, minor, core=core):
+            x, y = (major, minor) if core == 0 else (minor, major)
+            return at(z, y, x, core)
+
+        first += [
+            [along(z, i, 2 * high + low) for i in side for low in pair] for z in range(depth) for high in pair
+        ]
+        second += [
+            [along(z * SIDE + near, i, 2 * high + low) for high in pair for near in side]
+            for z in range(far) for i in side for low in pair
+        ]
     far_zs = [[(i * SIDE + z) * SIDE + y for i in range(far)] for z in side for y in side]
     value = keep + lax.ppermute(send, "section", [(i, i ^ 1) for i in range(section)])
     value = scatter_sum(value, both, first)
     value = scatter_sum(value, both, second)
-    value = scatter_sum(value, "scen", near_zs)
     value = add_up(exchange(value, "scen", far_zs))
-    value = gather(value, "scen", near_zs)
     value = gather(value, both, second)
     value = gather(value, both, first)
     return gather(value, "section", cores)

time: 145 us -> 138 us (0.952)
  blocking collectives: 94.1 us -> 88 us
    all_to_all x5 -> x4, blocking collectives: 65.6 us -> 57.5 us  [exchange(): return lax.all_to_all(parts, axis, 0, 0, axis_index_groups=groups)]
    all_to_all x3 -> x2, blocking collectives: 28.5 us -> 30.5 us  [scatter_sum(): return add_up(lax.all_to_all(parts, axis, 0, 0, axis_index_groups=groups))]
where the time goes in v1:
time: 138 us
  blocking collectives  88 us (64%)
  Pallas kernels  37.6 us (27%)
  starting transfers between devices  6.6 us (5%)
  local copies, waits for them, and re-layouts  2.14 us (2%)
  waiting for transfers between devices  2.08 us (2%)
    all_to_all x4, blocking collectives, exchange(): return lax.all_to_all(parts, axis, 0, 0, axis_index_groups=groups)  57.5 us
    all_to_all x2, blocking collectives, scatter_sum(): return add_up(lax.all_to_all(parts, axis, 0, 0, axis_index_groups=groups))  30.5 us
    pallas_call x1, Pallas kernels, first_solve(): pl.pallas_call(functools.partial(solve_kernel, blocks), out_shape=jax.Sha...  29 us
    pallas_call x1, Pallas kernels, local(): pl.pallas_call(functools.partial(terms_kernel, blocks), grid=(capacity,),...  7.85 us
    ppermute x1, starting transfers between devices, sum_over_devices(): lax.ppermute(send, 'section', [(i, i ^ 1) for i in range(section)])  6.6 us
  transfers between devices with their start and end apart: 1, of which 1 were waited for; matrix products, arithmetic and copies ran while one was open for 0% of the time, Pallas kernels for 0%

profile of v1, /device:TPU:1, one launch (start us, length us, event | category | flops | bytes accessed | tf_op | source)
XLA Modules:
  0.0 138.0 jit_solution(3893332862688328070)
XLA Ops:
  1.3 0.7 broadcast_in_dim.33.first_ref
  2.0 0.1 pad_add_fusion.place_ref
  2.0 7.9 %schur_terms.1 = (f32[1792,128]{1,0:T(8,128)S(1)}, f32[1792,128]{1,0:T(8,128)S(1)}, bf16[3,896,512]{2,1,0:T(8,128)(2,1)S(1)}, f32[3,1,512]{2,1,0:T(1,128)S(1)}) custom-call(s32[1]{0:T(128)S(6)} %copy.12.live_ref, s32[2]{0:T(128)S(1)} %pad_add_fusion.place_ref, s32[3,7]{1,0:T(4,128)} %mask_hbm.1, bf16[3,512,512]{2,1,0:T(8,128)(2,1)} %inverse_hbm.1, ...), custom_call_target="tpu_custom_call" | custom-call | tf_op jit(solution)/shard_map/schur_terms/pallas_call | solution.py:402
  9.9 6.6 %collective-permute-start = (f32[1792,128]{1,0:T(8,128)S(1)}, f32[1792,128]{1,0:T(8,128)S(1)}, u32[]{:S(2)}, u32[]{:S(2)}) collective-permute-start(f32[1792,128]{1,0:T(8,128)S(1)} %get-tuple-element.7), channel_id=1, source_target_pairs={{0,1},{1,0},{2,3},{3,2},{4,5},{5,4},{6,7},{7,6},{8,9},{9,8},{10,11... | collective-permute-start | bytes 2752520 | tf_op jit(solution)/shard_map/ppermute | solution.py:276
  16.5 2.1 %collective-permute-done = f32[1792,128]{1,0:T(8,128)S(1)} collective-permute-done((f32[1792,128]{1,0:T(8,128)S(1)}, f32[1792,128]{1,0:T(8,128)S(1)}, u32[]{:S(2)}, u32[]{:S(2)}) %collective-permute-start) | collective-permute-done | bytes 917536 | tf_op jit(solution)/shard_map/ppermute | solution.py:276
  18.6 0.1 add.77
  18.7 15.4 %all_to_all.30 = f32[8,224,128]{2,1,0:T(8,128)S(1)} all-to-all(f32[8,224,128]{2,1,0:T(8,128)S(1)} %bitcast.13), channel_id=1, replica_groups={{0,8,2,10,4,12,6,14},{16,24,18,26,20,28,22,30},{32,40,34,42,36,44,38,46..., dimensions={0} | all-to-all | bytes 1835008 | tf_op jit(solution)/shard_map/all_to_all | solution.py:238
  34.1 15.2 %all_to_all.31 = f32[8,28,128]{2,1,0:T(8,128)S(1)} all-to-all(f32[8,28,128]{2,1,0:T(8,128)S(1)} %reshape.29), channel_id=1, replica_groups={{0,32,64,96,16,48,80,112},{8,40,72,104,24,56,88,120},{2,34,66,98,18,50,..., dimensions={0} | all-to-all | bytes 229376 | tf_op jit(solution)/shard_map/all_to_all | solution.py:238
  49.3 25.8 %all_to_all.32 = f32[4,28,128]{2,1,0:T(8,128)S(1)} all-to-all(f32[4,28,128]{2,1,0:T(8,128)S(1)} %broadcast_in_dim.35), channel_id=1, replica_groups={{0,128,256,384},{8,136,264,392},{16,144,272,400},{24,152,280,408},{32,1..., dimensions={0} | all-to-all | bytes 114688 | tf_op jit(solution)/shard_map/all_to_all | solution.py:243
  75.1 10.4 %all_to_all.33 = f32[8,28,128]{2,1,0:T(8,128)S(1)} all-to-all(f32[8,28,128]{2,1,0:T(8,128)S(1)} %broadcast_in_dim.37), channel_id=1, replica_groups={{0,32,64,96,16,48,80,112},{8,40,72,104,24,56,88,120},{2,34,66,98,18,50,..., dimensions={0} | all-to-all | bytes 229376 | tf_op jit(solution)/shard_map/all_to_all | solution.py:243
  85.5 0.1 broadcast_in_dim.39
  85.6 15.9 %all_to_all.34 = f32[8,224,128]{2,1,0:T(8,128)S(1)} all-to-all(f32[8,224,128]{2,1,0:T(8,128)S(1)} %broadcast_in_dim.39), channel_id=1, replica_groups={{0,8,2,10,4,12,6,14},{16,24,18,26,20,28,22,30},{32,40,34,42,36,44,38,46..., dimensions={0} | all-to-all | bytes 1835008 | tf_op jit(solution)/shard_map/all_to_all | solution.py:243
  101.5 0.1 broadcast_in_dim.41
  101.6 5.4 %all_to_all.35 = f32[2,1792,128]{2,1,0:T(8,128)S(1)} all-to-all(f32[2,1792,128]{2,1,0:T(8,128)S(1)} %broadcast_in_dim.41), channel_id=1, replica_groups={{0,1},{2,3},{4,5},{6,7},{8,9},{10,11},{12,13},{14,15},{16,17},{18,19},{..., dimensions={0} | all-to-all | bytes 3670016 | tf_op jit(solution)/shard_map/all_to_all | solution.py:243
  107.0 29.0 %first_solve.1.step_ref = f32[8,896]{1,0:T(8,128)S(1)} custom-call(f32[3584,128]{1,0:T(8,128)S(1)} %bitcast.12), custom_call_target="tpu_custom_call" | custom-call | tf_op jit(solution)/shard_map/first_solve/pallas_call | solution.py:355
  136.0 0.6 slice_reduce_fusion
  136.6 0.8 scen_steps.1
  137.4 0.6 copy.11
  (7 shorter events, 0.1 us)
Async XLA Ops:
  9.9 8.7 %collective-permute-start = (f32[1792,128]{1,0:T(8,128)S(1)}, f32[1792,128]{1,0:T(8,128)S(1)}, u32[]{:S(2)}, u32[]{:S(2)}) collective-permute-start(f32[1792,128]{1,0:T(8,128)S(1)} %get-tuple-element.7), channel_id=1, source_target_pairs={{0,1},{1,0},{2,3},{3,2},{4,5},{5,4},{6,7},{7,6},{8,9},{9,8},{10,11... | collective-permute-start | bytes 2752520 | tf_op jit(solution)/shard_map/ppermute | solution.py:276

commit v2 on v1

--- a/solution.py
+++ b/solution.py
@@ -256,7 +256,6 @@
     def at(z, y, x, core):
         return (z * SIDE + y) * section + 2 * x + core
 
-    cores = [[2 * i, 2 * i + 1] for i in range(SIDE)]
     side, pair = range(SIDE), range(2)
     first, second = [], []
     for core in range(2):
@@ -279,18 +278,24 @@
     value = add_up(exchange(value, "scen", far_zs))
     value = gather(value, both, second)
     value = gather(value, both, first)
-    return gather(value, "section", cores)
-
-
-def solve_kernel(blocks, packed_ref, step_ref, work_ref, inverse_ref, turned_ref, rhs_ref, z_ref, x_ref):
+    return value, lax.ppermute(value, "section", [(i, i ^ 1) for i in range(section)])
+
+
+def solve_kernel(blocks, core_ref, own_ref, other_ref, step_ref, work_ref, inverse_ref, turned_ref, rhs_ref, z_ref, x_ref):
     row = lax.broadcasted_iota(jnp.int32, (LANES, LANES), 0)
     column = lax.broadcasted_iota(jnp.int32, (LANES, LANES), 1)
     half = LANES // 2
     left_half = lax.broadcasted_iota(jnp.int32, (1, LANES), 1) < half
     scales, scale_columns = [], []
+    height = own_ref.shape[0]
+
+    def packed(base):
+        at = slice(base % height, base % height + LANES)
+        return jnp.where(core_ref[0] == base // height, own_ref[at, :], other_ref[at, :])
+
     for j in range(blocks):
         base = panel_base(j, blocks)
-        square = packed_ref[base : base + LANES, :]
+        square = packed(base)
         scale = lax.rsqrt(jnp.sum(jnp.where(row == column, square, 0.0), axis=0, keepdims=True))
         scales.append(scale)
         scale_columns.append(jnp.sum(jnp.where(row == column, scale, 0.0), axis=1, keepdims=True))
@@ -300,7 +305,7 @@
     for j in range(blocks):
         for i in range(j, blocks):
             base = panel_base(j, blocks) + (i - j) * LANES
-            square = packed_ref[base : base + LANES, :] * scale_columns[i] * scales[j]
+            square = packed(base) * scale_columns[i] * scales[j]
             if i == j:
                 square = jnp.where(row >= column, square, square.T)
             work_ref[base : base + LANES, :] = square
@@ -321,16 +326,24 @@
                 z_ref[jj] = z
                 if rest == 0:
                     return
-                panel = work_ref[at + LANES : at + (rest + 1) * LANES, :]
-                turned = mixed(panel, inverse)
+                panel_high, panel_low = halves(work_ref[at + LANES : at + (rest + 1) * LANES, :])
+                high, low = halves(inverse)
+                turned = dot(
+                    jnp.concatenate([panel_high, panel_low, panel_high], axis=1),
+                    jnp.concatenate([high, high, low], axis=0),
+                )
                 turned_ref[at + LANES : at + (rest + 1) * LANES, :] = turned
-                for s in range(rest):
-                    left = jnp.concatenate([turned[s * LANES :, :], z], axis=0)
-                    change = mixed_rows(left, panel[s * LANES : (s + 1) * LANES, :])
-                    height = (rest - s) * LANES
-                    target = panel_base(jj + 1 + s, blocks)
-                    work_ref[target : target + height, :] -= change[:height]
-                    rhs_ref[jj + 1 + s] -= change[height:]
+                high, low = halves(jnp.concatenate([turned, z, z], axis=0))
+                left = jnp.concatenate([high, low, high], axis=1)
+                right = jnp.concatenate([panel_high, panel_high, panel_low], axis=1)
+                for s in range(0, rest, 2):
+                    change = dot_rows(left[s * LANES :], right[s * LANES : min(s + 2, rest) * LANES])
+                    for t in range(s, min(s + 2, rest)):
+                        own = change[(t - s) * LANES :, (t - s) * LANES : (t - s + 1) * LANES]
+                        height = (rest - t) * LANES
+                        target = panel_base(jj + 1 + t, blocks)
+                        work_ref[target : target + height, :] -= own[:height]
+                        rhs_ref[jj + 1 + t] -= own[height : height + SUBLANES]
 
         return carry
 
@@ -347,28 +360,28 @@
         step_ref[:, at] = x_ref[:, at] * scales[j]
 
 
-def first_solve(packed):
-    blocks = 0
-    while panel_base(blocks, blocks) < packed.shape[0]:
-        blocks += 1
+def first_solve(blocks, core, own, other):
+    rows = panel_base(blocks, blocks)
+    vmem = pl.BlockSpec(memory_space=pltpu.VMEM)
     square = (LANES, LANES)
     return pl.pallas_call(
         functools.partial(solve_kernel, blocks),
+        in_specs=[pl.BlockSpec(memory_space=pltpu.SMEM), vmem, vmem],
         out_shape=jax.ShapeDtypeStruct((SUBLANES, blocks * LANES), F32),
         scratch_shapes=[
-            pltpu.VMEM((packed.shape[0], LANES), F32),
+            pltpu.VMEM((rows, LANES), F32),
             pltpu.VMEM(square, F32),
-            pltpu.VMEM((packed.shape[0], LANES), F32),
+            pltpu.VMEM((rows, LANES), F32),
             pltpu.VMEM((blocks, SUBLANES, LANES), F32),
             pltpu.VMEM((blocks, SUBLANES, LANES), F32),
             pltpu.VMEM((SUBLANES, blocks * LANES), F32),
         ],
         compiler_params=pltpu.CompilerParams(vmem_limit_bytes=48 * 1024 * 1024),
         name="first_solve",
-    )(packed)
-
-
-def finish_kernel(live_ref, step_ref, product_ref, reduced_ref, out_ref):
+    )(core, own, other)
+
+
+def finish_kernel(live_ref, step_ref, product_ref, reduced_ref, first_ref, out_ref):
     slot = pl.program_id(0)
     first = step_ref[0:1, :]
     high, rest = halves(first)
@@ -378,7 +391,8 @@
         row == 0, high.astype(F32), jnp.where(row == 1, middle.astype(F32), jnp.where(row == 2, low.astype(F32), 0.0))
     ).astype(BF16)
     moved = jnp.sum(dot(pieces, product_ref[0]), axis=0, keepdims=True)
-    out_ref[0] = jnp.where(slot < live_ref[0], reduced_ref[0] - moved, 0.0)
+    out_ref[pl.ds(slot, 1), :] = jnp.where(slot < live_ref[0], reduced_ref[0] - moved, 0.0)
+    first_ref[...] = first[0]
 
 
 def local(scen_inverse, link_border, scen_rhs, link_mask, live_slots, first_block, first_rhs):
@@ -438,18 +452,20 @@
         live_slots, place, in_hbm(link_mask), in_hbm(scen_inverse), link_border, in_hbm(scen_rhs), in_hbm(first_block),
         first_rhs[None, :],
     )
-    packed = sum_over_devices(keep, send)
-    step = first_solve(packed)
-    scen_step = pl.pallas_call(
+    own, other = sum_over_devices(keep, send)
+    step = first_solve(blocks, lax.rem(place[1:2], 2), own, other)
+    return pl.pallas_call(
         finish_kernel,
         grid=(capacity,),
         in_specs=[smem, whole(SUBLANES, link_width), per_slot(link_width, scen_width), per_slot(1, scen_width)],
-        out_specs=per_slot(1, scen_width),
-        out_shape=jax.ShapeDtypeStruct((capacity, 1, scen_width), F32),
+        out_specs=[whole(link_width), whole(capacity, scen_width)],
+        out_shape=[
+            jax.ShapeDtypeStruct((link_width,), F32),
+            jax.ShapeDtypeStruct((capacity, scen_width), F32),
+        ],
         compiler_params=pltpu.CompilerParams(vmem_limit_bytes=48 * 1024 * 1024),
         name="scen_steps",
     )(live_slots, step, product, reduced)
-    return step[0], scen_step[:, 0, :]
 
 
 def solution(mesh):

time: 138 us -> 136 us (0.986)
  blocking collectives: 88 us -> 80.2 us
  starting transfers between devices: 6.6 us -> 13.3 us
  Pallas kernels: 37.6 us -> 35.5 us
  waiting for transfers between devices: 2.08 us -> 4.15 us
    all_to_all x4 -> x3, blocking collectives: 57.5 us -> 48.2 us  [exchange(): return lax.all_to_all(parts, axis, 0, 0, axis_index_groups=groups)]
    ppermute x0 -> x1, starting transfers between devices: none -> 4.57 us  [sum_over_devices(): lax.ppermute(value, 'section', [(i, i ^ 1) for i in range(section)])]
    pallas_call x1, Pallas kernels: 7.85 us -> 5.68 us  [local(): pl.pallas_call(functools.partial(terms_kernel, blocks), grid=(capacity,),...]
    ppermute x1, starting transfers between devices: 6.6 us -> 8.77 us  [sum_over_devices(): lax.ppermute(send, 'section', [(i, i ^ 1) for i in range(section)])]
    ppermute x0 -> x1, waiting for transfers between devices: none -> 2.07 us  [sum_over_devices(): lax.ppermute(value, 'section', [(i, i ^ 1) for i in range(section)])]
    all_to_all x2, blocking collectives: 30.5 us -> 32 us  [scatter_sum(): return add_up(lax.all_to_all(parts, axis, 0, 0, axis_index_groups=groups))]
  transfers between devices with their start and end apart: 1 -> 2, of which waited for: 1 -> 2; matrix products, arithmetic and copies ran while one was open for 0% -> 0% of each run, Pallas kernels for 0% -> 0%
where the time goes in v2:
time: 136 us
  blocking collectives  80.2 us (59%)
  Pallas kernels  35.5 us (26%)
  starting transfers between devices  13.3 us (10%)
  waiting for transfers between devices  4.15 us (3%)
    all_to_all x3, blocking collectives, exchange(): return lax.all_to_all(parts, axis, 0, 0, axis_index_groups=groups)  48.2 us
    all_to_all x2, blocking collectives, scatter_sum(): return add_up(lax.all_to_all(parts, axis, 0, 0, axis_index_groups=groups))  32 us
    pallas_call x1, Pallas kernels, first_solve(): pl.pallas_call(functools.partial(solve_kernel, blocks), in_specs=[pl.Bloc...  28.4 us
    ppermute x1, starting transfers between devices, sum_over_devices(): lax.ppermute(send, 'section', [(i, i ^ 1) for i in range(section)])  8.77 us
    pallas_call x1, Pallas kernels, local(): pl.pallas_call(functools.partial(terms_kernel, blocks), grid=(capacity,),...  5.68 us
    ppermute x1, starting transfers between devices, sum_over_devices(): lax.ppermute(value, 'section', [(i, i ^ 1) for i in range(section)])  4.57 us
  transfers between devices with their start and end apart: 2, of which 2 were waited for; matrix products, arithmetic and copies ran while one was open for 0% of the time, Pallas kernels for 0%

profile of v2, /device:TPU:1, one launch (start us, length us, event | category | flops | bytes accessed | tf_op | source)
XLA Modules:
  0.0 135.6 jit_solution(13070749535410451458)
XLA Ops:
  1.3 0.7 broadcast_in_dim.26.first_ref
  2.0 0.1 pad_add_fusion.place_ref
  2.0 5.7 %schur_terms.1 = (f32[1792,128]{1,0:T(8,128)S(1)}, f32[1792,128]{1,0:T(8,128)S(1)}, bf16[3,896,512]{2,1,0:T(8,128)(2,1)S(1)}, f32[3,1,512]{2,1,0:T(1,128)S(1)}) custom-call(s32[1]{0:T(128)S(6)} %copy.9.live_ref, s32[2]{0:T(128)S(1)} %pad_add_fusion.place_ref, s32[3,7]{1,0:T(4,128)} %mask_hbm.1, bf16[3,512,512]{2,1,0:T(8,128)(2,1)} %inverse_hbm.1, ...), custom_call_target="tpu_custom_call" | custom-call | tf_op jit(solution)/shard_map/schur_terms/pallas_call | solution.py:416
  7.7 8.8 %collective-permute-start = (f32[1792,128]{1,0:T(8,128)S(1)}, f32[1792,128]{1,0:T(8,128)S(1)}, u32[]{:S(2)}, u32[]{:S(2)}) collective-permute-start(f32[1792,128]{1,0:T(8,128)S(1)} %get-tuple-element.7), channel_id=1, source_target_pairs={{0,1},{1,0},{2,3},{3,2},{4,5},{5,4},{6,7},{7,6},{8,9},{9,8},{10,11... | collective-permute-start | bytes 2752520 | tf_op jit(solution)/shard_map/ppermute | solution.py:275
  16.5 2.1 %collective-permute-done = f32[1792,128]{1,0:T(8,128)S(1)} collective-permute-done((f32[1792,128]{1,0:T(8,128)S(1)}, f32[1792,128]{1,0:T(8,128)S(1)}, u32[]{:S(2)}, u32[]{:S(2)}) %collective-permute-start) | collective-permute-done | bytes 917536 | tf_op jit(solution)/shard_map/ppermute | solution.py:275
  18.6 0.1 add.77
  18.7 16.9 %all_to_all.25 = f32[8,224,128]{2,1,0:T(8,128)S(1)} all-to-all(f32[8,224,128]{2,1,0:T(8,128)S(1)} %bitcast.10), channel_id=1, replica_groups={{0,8,2,10,4,12,6,14},{16,24,18,26,20,28,22,30},{32,40,34,42,36,44,38,46..., dimensions={0} | all-to-all | bytes 1835008 | tf_op jit(solution)/shard_map/all_to_all | solution.py:238
  35.7 15.1 %all_to_all.26 = f32[8,28,128]{2,1,0:T(8,128)S(1)} all-to-all(f32[8,28,128]{2,1,0:T(8,128)S(1)} %reshape.30), channel_id=1, replica_groups={{0,32,64,96,16,48,80,112},{8,40,72,104,24,56,88,120},{2,34,66,98,18,50,..., dimensions={0} | all-to-all | bytes 229376 | tf_op jit(solution)/shard_map/all_to_all | solution.py:238
  50.8 23.0 %all_to_all.27 = f32[4,28,128]{2,1,0:T(8,128)S(1)} all-to-all(f32[4,28,128]{2,1,0:T(8,128)S(1)} %broadcast_in_dim.28), channel_id=1, replica_groups={{0,128,256,384},{8,136,264,392},{16,144,272,400},{24,152,280,408},{32,1..., dimensions={0} | all-to-all | bytes 114688 | tf_op jit(solution)/shard_map/all_to_all | solution.py:243
  73.8 10.4 %all_to_all.28 = f32[8,28,128]{2,1,0:T(8,128)S(1)} all-to-all(f32[8,28,128]{2,1,0:T(8,128)S(1)} %broadcast_in_dim.30), channel_id=1, replica_groups={{0,32,64,96,16,48,80,112},{8,40,72,104,24,56,88,120},{2,34,66,98,18,50,..., dimensions={0} | all-to-all | bytes 229376 | tf_op jit(solution)/shard_map/all_to_all | solution.py:243
  84.2 0.1 broadcast_in_dim.32
  84.2 14.9 %all_to_all.29 = f32[8,224,128]{2,1,0:T(8,128)S(1)} all-to-all(f32[8,224,128]{2,1,0:T(8,128)S(1)} %broadcast_in_dim.32), channel_id=1, replica_groups={{0,8,2,10,4,12,6,14},{16,24,18,26,20,28,22,30},{32,40,34,42,36,44,38,46..., dimensions={0} | all-to-all | bytes 1835008 | tf_op jit(solution)/shard_map/all_to_all | solution.py:243
  99.1 4.6 %collective-permute-start.1 = (f32[1792,128]{1,0:T(8,128)S(1)}, f32[1792,128]{1,0:T(8,128)S(1)}, u32[]{:S(2)}, u32[]{:S(2)}) collective-permute-start(f32[1792,128]{1,0:T(8,128)S(1)} %bitcast.8), channel_id=1, source_target_pairs={{0,1},{1,0},{2,3},{3,2},{4,5},{5,4},{6,7},{7,6},{8,9},{9,8},{10,11... | collective-permute-start | bytes 2752520 | tf_op jit(solution)/shard_map/ppermute | solution.py:281
  103.7 2.1 %collective-permute-done.1.other_ref = f32[1792,128]{1,0:T(8,128)S(1)} collective-permute-done((f32[1792,128]{1,0:T(8,128)S(1)}, f32[1792,128]{1,0:T(8,128)S(1)}, u32[]{:S(2)}, u32[]{:S(2)}) %collective-permute-start.1) | collective-permute-done | bytes 917536 | tf_op jit(solution)/shard_map/ppermute | solution.py:281
  105.8 28.4 %first_solve.1.step_ref = f32[8,896]{1,0:T(8,128)S(1)} custom-call(s32[1]{0:T(128)S(6)} %rem.18.core_ref, f32[1792,128]{1,0:T(8,128)S(1)} %bitcast.9, f32[1792,128]{1,0:T(8,128)S(1)} %collective-permute-done.1.other_ref), custom_call_target="tpu_custom_call" | custom-call | tf_op jit(solution)/shard_map/first_solve/pallas_call | solution.py:367
  134.2 1.4 %scen_steps.1 = (f32[896]{0:T(1024)}, f32[3,512]{1,0:T(4,128)}) custom-call(s32[1]{0:T(128)S(6)} %copy.9.live_ref, f32[8,896]{1,0:T(8,128)S(1)} %first_solve.1.step_ref, bf16[3,896,512]{2,1,0:T(8,128)(2,1)S(1)} %get-tuple-element.8.product_ref, f32[3,1,512]{2,1,0:T(1,128)S(1)} %get-tuple-element.9.reduced_ref), custom_call_target="tpu_custom_call" | custom-call | tf_op jit(solution)/shard_map/scen_steps/pallas_call | solution.py:457
  (7 shorter events, 0.1 us)
Async XLA Ops:
  7.7 10.9 %collective-permute-start = (f32[1792,128]{1,0:T(8,128)S(1)}, f32[1792,128]{1,0:T(8,128)S(1)}, u32[]{:S(2)}, u32[]{:S(2)}) collective-permute-start(f32[1792,128]{1,0:T(8,128)S(1)} %get-tuple-element.7), channel_id=1, source_target_pairs={{0,1},{1,0},{2,3},{3,2},{4,5},{5,4},{6,7},{7,6},{8,9},{9,8},{10,11... | collective-permute-start | bytes 2752520 | tf_op jit(solution)/shard_map/ppermute | solution.py:275
  99.1 6.7 %collective-permute-start.1 = (f32[1792,128]{1,0:T(8,128)S(1)}, f32[1792,128]{1,0:T(8,128)S(1)}, u32[]{:S(2)}, u32[]{:S(2)}) collective-permute-start(f32[1792,128]{1,0:T(8,128)S(1)} %bitcast.8), channel_id=1, source_target_pairs={{0,1},{1,0},{2,3},{3,2},{4,5},{5,4},{6,7},{7,6},{8,9},{9,8},{10,11... | collective-permute-start | bytes 2752520 | tf_op jit(solution)/shard_map/ppermute | solution.py:281

commit v3 on v2

--- a/solution.py
+++ b/solution.py
@@ -8,7 +8,7 @@
 from jax.sharding import PartitionSpec as P
 
 SIDE = 4
-STRIP = 4
+STRIP = 8
 LANES = 128
 SUBLANES = 8
 F32 = jnp.float32
@@ -91,7 +91,7 @@
             pl.ds(pl.multiple_of(col_base, LANES), corner_wide_ref.shape[1]),
         ] = moved
         at_origin = jnp.logical_and(place_ref[0] == 0, place_ref[1] == 0)
-        rhs_ref[...] = jnp.where(at_origin, first_ref[...], 0.0)
+        rhs_ref[...] = jnp.where(at_origin, first_ref[...][None, :], 0.0)
 
     fetch(slot).wait()
 
@@ -420,7 +420,7 @@
             smem, smem, hbm, hbm,
             per_slot(scen_width, link_width),
             hbm, hbm,
-            whole(1, link_width),
+            whole(link_width),
         ],
         out_specs=[
             whole(packed_rows // 2, LANES),
@@ -450,7 +450,7 @@
         name="schur_terms",
     )(
         live_slots, place, in_hbm(link_mask), in_hbm(scen_inverse), link_border, in_hbm(scen_rhs), in_hbm(first_block),
-        first_rhs[None, :],
+        in_hbm(first_rhs),
     )
     own, other = sum_over_devices(keep, send)
     step = first_solve(blocks, lax.rem(place[1:2], 2), own, other)

time: 136 us -> 137 us (level)
  starting transfers between devices: 13.3 us -> 9.13 us
  Pallas kernels: 35.5 us -> 38.8 us
  blocking collectives: 80.2 us -> 83.1 us
    all_to_all x3, blocking collectives: 48.2 us -> 50.9 us  [exchange(): return lax.all_to_all(parts, axis, 0, 0, axis_index_groups=groups)]
    pallas_call x1, Pallas kernels: 5.68 us -> 7.87 us  [local(): pl.pallas_call(functools.partial(terms_kernel, blocks), grid=(capacity,),...]
    ppermute x1, starting transfers between devices: 8.77 us -> 6.6 us  [sum_over_devices(): lax.ppermute(send, 'section', [(i, i ^ 1) for i in range(section)])]
    ppermute x1, starting transfers between devices: 4.57 us -> 2.53 us  [sum_over_devices(): lax.ppermute(value, 'section', [(i, i ^ 1) for i in range(section)])]
where the time goes in v3:
time: 137 us
  blocking collectives  83.1 us (61%)
  Pallas kernels  38.8 us (28%)
  starting transfers between devices  9.13 us (7%)
  waiting for transfers between devices  4.15 us (3%)
    all_to_all x3, blocking collectives, exchange(): return lax.all_to_all(parts, axis, 0, 0, axis_index_groups=groups)  50.9 us
    all_to_all x2, blocking collectives, scatter_sum(): return add_up(lax.all_to_all(parts, axis, 0, 0, axis_index_groups=groups))  32.2 us
    pallas_call x1, Pallas kernels, first_solve(): pl.pallas_call(functools.partial(solve_kernel, blocks), in_specs=[pl.Bloc...  29.6 us
    pallas_call x1, Pallas kernels, local(): pl.pallas_call(functools.partial(terms_kernel, blocks), grid=(capacity,),...  7.87 us
    ppermute x1, starting transfers between devices, sum_over_devices(): lax.ppermute(send, 'section', [(i, i ^ 1) for i in range(section)])  6.6 us
  transfers between devices with their start and end apart: 2, of which 2 were waited for; matrix products, arithmetic and copies ran while one was open for 0% of the time, Pallas kernels for 0%

profile of v3, /device:TPU:1, one launch (start us, length us, event | category | flops | bytes accessed | tf_op | source)
XLA Modules:
  0.0 136.9 jit_solution(12505126900830435426)
XLA Ops:
  1.3 0.1 pad_add_fusion.place_ref
  1.4 7.9 %schur_terms.1 = (f32[1792,128]{1,0:T(8,128)S(1)}, f32[1792,128]{1,0:T(8,128)S(1)}, bf16[3,896,512]{2,1,0:T(8,128)(2,1)S(1)}, f32[3,1,512]{2,1,0:T(1,128)S(1)}) custom-call(s32[1]{0:T(128)S(6)} %copy.9.live_ref, s32[2]{0:T(128)S(1)} %pad_add_fusion.place_ref, s32[3,7]{1,0:T(4,128)} %mask_hbm.1, bf16[3,512,512]{2,1,0:T(8,128)(2,1)} %inverse_hbm.1, ...), custom_call_target="tpu_custom_call" | custom-call | tf_op jit(solution)/shard_map/schur_terms/pallas_call | solution.py:416
  9.2 6.6 %collective-permute-start = (f32[1792,128]{1,0:T(8,128)S(1)}, f32[1792,128]{1,0:T(8,128)S(1)}, u32[]{:S(2)}, u32[]{:S(2)}) collective-permute-start(f32[1792,128]{1,0:T(8,128)S(1)} %get-tuple-element.7), channel_id=1, source_target_pairs={{0,1},{1,0},{2,3},{3,2},{4,5},{5,4},{6,7},{7,6},{8,9},{9,8},{10,11... | collective-permute-start | bytes 2752520 | tf_op jit(solution)/shard_map/ppermute | solution.py:275
  15.8 2.1 %collective-permute-done = f32[1792,128]{1,0:T(8,128)S(1)} collective-permute-done((f32[1792,128]{1,0:T(8,128)S(1)}, f32[1792,128]{1,0:T(8,128)S(1)}, u32[]{:S(2)}, u32[]{:S(2)}) %collective-permute-start) | collective-permute-done | bytes 917536 | tf_op jit(solution)/shard_map/ppermute | solution.py:275
  17.9 0.1 add.77
  18.0 16.5 %all_to_all.25 = f32[8,224,128]{2,1,0:T(8,128)S(1)} all-to-all(f32[8,224,128]{2,1,0:T(8,128)S(1)} %bitcast.10), channel_id=1, replica_groups={{0,8,2,10,4,12,6,14},{16,24,18,26,20,28,22,30},{32,40,34,42,36,44,38,46..., dimensions={0} | all-to-all | bytes 1835008 | tf_op jit(solution)/shard_map/all_to_all | solution.py:238
  34.5 15.8 %all_to_all.26 = f32[8,28,128]{2,1,0:T(8,128)S(1)} all-to-all(f32[8,28,128]{2,1,0:T(8,128)S(1)} %reshape.30), channel_id=1, replica_groups={{0,32,64,96,16,48,80,112},{8,40,72,104,24,56,88,120},{2,34,66,98,18,50,..., dimensions={0} | all-to-all | bytes 229376 | tf_op jit(solution)/shard_map/all_to_all | solution.py:238
  50.3 24.4 %all_to_all.27 = f32[4,28,128]{2,1,0:T(8,128)S(1)} all-to-all(f32[4,28,128]{2,1,0:T(8,128)S(1)} %broadcast_in_dim.24), channel_id=1, replica_groups={{0,128,256,384},{8,136,264,392},{16,144,272,400},{24,152,280,408},{32,1..., dimensions={0} | all-to-all | bytes 114688 | tf_op jit(solution)/shard_map/all_to_all | solution.py:243
  74.7 10.3 %all_to_all.28 = f32[8,28,128]{2,1,0:T(8,128)S(1)} all-to-all(f32[8,28,128]{2,1,0:T(8,128)S(1)} %broadcast_in_dim.26), channel_id=1, replica_groups={{0,32,64,96,16,48,80,112},{8,40,72,104,24,56,88,120},{2,34,66,98,18,50,..., dimensions={0} | all-to-all | bytes 229376 | tf_op jit(solution)/shard_map/all_to_all | solution.py:243
  85.0 0.1 broadcast_in_dim.28
  85.1 16.2 %all_to_all.29 = f32[8,224,128]{2,1,0:T(8,128)S(1)} all-to-all(f32[8,224,128]{2,1,0:T(8,128)S(1)} %broadcast_in_dim.28), channel_id=1, replica_groups={{0,8,2,10,4,12,6,14},{16,24,18,26,20,28,22,30},{32,40,34,42,36,44,38,46..., dimensions={0} | all-to-all | bytes 1835008 | tf_op jit(solution)/shard_map/all_to_all | solution.py:243
  101.3 2.5 %collective-permute-start.1 = (f32[1792,128]{1,0:T(8,128)S(1)}, f32[1792,128]{1,0:T(8,128)S(1)}, u32[]{:S(2)}, u32[]{:S(2)}) collective-permute-start(f32[1792,128]{1,0:T(8,128)S(1)} %bitcast.8), channel_id=1, source_target_pairs={{0,1},{1,0},{2,3},{3,2},{4,5},{5,4},{6,7},{7,6},{8,9},{9,8},{10,11... | collective-permute-start | bytes 2752520 | tf_op jit(solution)/shard_map/ppermute | solution.py:281
  103.8 2.1 %collective-permute-done.1.other_ref = f32[1792,128]{1,0:T(8,128)S(1)} collective-permute-done((f32[1792,128]{1,0:T(8,128)S(1)}, f32[1792,128]{1,0:T(8,128)S(1)}, u32[]{:S(2)}, u32[]{:S(2)}) %collective-permute-start.1) | collective-permute-done | bytes 917536 | tf_op jit(solution)/shard_map/ppermute | solution.py:281
  105.9 29.6 %first_solve.1.step_ref = f32[8,896]{1,0:T(8,128)S(1)} custom-call(s32[1]{0:T(128)S(6)} %rem.18.core_ref, f32[1792,128]{1,0:T(8,128)S(1)} %bitcast.9, f32[1792,128]{1,0:T(8,128)S(1)} %collective-permute-done.1.other_ref), custom_call_target="tpu_custom_call" | custom-call | tf_op jit(solution)/shard_map/first_solve/pallas_call | solution.py:367
  135.5 1.4 %scen_steps.1 = (f32[896]{0:T(1024)}, f32[3,512]{1,0:T(4,128)}) custom-call(s32[1]{0:T(128)S(6)} %copy.9.live_ref, f32[8,896]{1,0:T(8,128)S(1)} %first_solve.1.step_ref, bf16[3,896,512]{2,1,0:T(8,128)(2,1)S(1)} %get-tuple-element.8.product_ref, f32[3,1,512]{2,1,0:T(1,128)S(1)} %get-tuple-element.9.reduced_ref), custom_call_target="tpu_custom_call" | custom-call | tf_op jit(solution)/shard_map/scen_steps/pallas_call | solution.py:457
  (7 shorter events, 0.1 us)
Async XLA Ops:
  9.2 8.7 %collective-permute-start = (f32[1792,128]{1,0:T(8,128)S(1)}, f32[1792,128]{1,0:T(8,128)S(1)}, u32[]{:S(2)}, u32[]{:S(2)}) collective-permute-start(f32[1792,128]{1,0:T(8,128)S(1)} %get-tuple-element.7), channel_id=1, source_target_pairs={{0,1},{1,0},{2,3},{3,2},{4,5},{5,4},{6,7},{7,6},{8,9},{9,8},{10,11... | collective-permute-start | bytes 2752520 | tf_op jit(solution)/shard_map/ppermute | solution.py:275
  101.3 4.6 %collective-permute-start.1 = (f32[1792,128]{1,0:T(8,128)S(1)}, f32[1792,128]{1,0:T(8,128)S(1)}, u32[]{:S(2)}, u32[]{:S(2)}) collective-permute-start(f32[1792,128]{1,0:T(8,128)S(1)} %bitcast.8), channel_id=1, source_target_pairs={{0,1},{1,0},{2,3},{3,2},{4,5},{5,4},{6,7},{7,6},{8,9},{9,8},{10,11... | collective-permute-start | bytes 2752520 | tf_op jit(solution)/shard_map/ppermute | solution.py:281

commit v4 on v3

--- a/solution.py
+++ b/solution.py
@@ -8,7 +8,7 @@
 from jax.sharding import PartitionSpec as P
 
 SIDE = 4
-STRIP = 8
+STRIP = 4
 LANES = 128
 SUBLANES = 8
 F32 = jnp.float32

time: 137 us -> 136 us (level)
  blocking collectives: 83.1 us -> 80.8 us
  starting transfers between devices: 9.13 us -> 11.4 us
    all_to_all x2, blocking collectives: 32.2 us -> 27.5 us  [scatter_sum(): return add_up(lax.all_to_all(parts, axis, 0, 0, axis_index_groups=groups))]
    all_to_all x3, blocking collectives: 50.9 us -> 53.4 us  [exchange(): return lax.all_to_all(parts, axis, 0, 0, axis_index_groups=groups)]
    ppermute x1, starting transfers between devices: 6.6 us -> 8.79 us  [sum_over_devices(): lax.ppermute(send, 'section', [(i, i ^ 1) for i in range(section)])]
where the time goes in v4:
time: 136 us
  blocking collectives  80.8 us (59%)
  Pallas kernels  37.7 us (28%)
  starting transfers between devices  11.4 us (8%)
  waiting for transfers between devices  4.15 us (3%)
    all_to_all x3, blocking collectives, exchange(): return lax.all_to_all(parts, axis, 0, 0, axis_index_groups=groups)  53.4 us
    pallas_call x1, Pallas kernels, first_solve(): pl.pallas_call(functools.partial(solve_kernel, blocks), in_specs=[pl.Bloc...  28.4 us
    all_to_all x2, blocking collectives, scatter_sum(): return add_up(lax.all_to_all(parts, axis, 0, 0, axis_index_groups=groups))  27.5 us
    ppermute x1, starting transfers between devices, sum_over_devices(): lax.ppermute(send, 'section', [(i, i ^ 1) for i in range(section)])  8.79 us
    pallas_call x1, Pallas kernels, local(): pl.pallas_call(functools.partial(terms_kernel, blocks), grid=(capacity,),...  7.87 us
  transfers between devices with their start and end apart: 2, of which 2 were waited for; matrix products, arithmetic and copies ran while one was open for 0% of the time, Pallas kernels for 0%

profile of v4, /device:TPU:1, one launch (start us, length us, event | category | flops | bytes accessed | tf_op | source)
XLA Modules:
  0.0 135.7 jit_solution(10303513665518968344)
XLA Ops:
  1.3 0.1 pad_add_fusion.place_ref
  1.4 7.9 %schur_terms.1 = (f32[1792,128]{1,0:T(8,128)S(1)}, f32[1792,128]{1,0:T(8,128)S(1)}, bf16[3,896,512]{2,1,0:T(8,128)(2,1)S(1)}, f32[3,1,512]{2,1,0:T(1,128)S(1)}) custom-call(s32[1]{0:T(128)S(6)} %copy.9.live_ref, s32[2]{0:T(128)S(1)} %pad_add_fusion.place_ref, s32[3,7]{1,0:T(4,128)} %mask_hbm.1, bf16[3,512,512]{2,1,0:T(8,128)(2,1)} %inverse_hbm.1, ...), custom_call_target="tpu_custom_call" | custom-call | tf_op jit(solution)/shard_map/schur_terms/pallas_call | solution.py:416
  9.2 8.8 %collective-permute-start = (f32[1792,128]{1,0:T(8,128)S(1)}, f32[1792,128]{1,0:T(8,128)S(1)}, u32[]{:S(2)}, u32[]{:S(2)}) collective-permute-start(f32[1792,128]{1,0:T(8,128)S(1)} %get-tuple-element.7), channel_id=1, source_target_pairs={{0,1},{1,0},{2,3},{3,2},{4,5},{5,4},{6,7},{7,6},{8,9},{9,8},{10,11... | collective-permute-start | bytes 2752520 | tf_op jit(solution)/shard_map/ppermute | solution.py:275
  18.0 2.1 %collective-permute-done = f32[1792,128]{1,0:T(8,128)S(1)} collective-permute-done((f32[1792,128]{1,0:T(8,128)S(1)}, f32[1792,128]{1,0:T(8,128)S(1)}, u32[]{:S(2)}, u32[]{:S(2)}) %collective-permute-start) | collective-permute-done | bytes 917536 | tf_op jit(solution)/shard_map/ppermute | solution.py:275
  20.1 0.1 add.77
  20.2 14.8 %all_to_all.25 = f32[8,224,128]{2,1,0:T(8,128)S(1)} all-to-all(f32[8,224,128]{2,1,0:T(8,128)S(1)} %bitcast.10), channel_id=1, replica_groups={{0,8,2,10,4,12,6,14},{16,24,18,26,20,28,22,30},{32,40,34,42,36,44,38,46..., dimensions={0} | all-to-all | bytes 1835008 | tf_op jit(solution)/shard_map/all_to_all | solution.py:238
  35.1 12.6 %all_to_all.26 = f32[8,28,128]{2,1,0:T(8,128)S(1)} all-to-all(f32[8,28,128]{2,1,0:T(8,128)S(1)} %reshape.30), channel_id=1, replica_groups={{0,32,64,96,16,48,80,112},{8,40,72,104,24,56,88,120},{2,34,66,98,18,50,..., dimensions={0} | all-to-all | bytes 229376 | tf_op jit(solution)/shard_map/all_to_all | solution.py:238
  47.8 26.9 %all_to_all.27 = f32[4,28,128]{2,1,0:T(8,128)S(1)} all-to-all(f32[4,28,128]{2,1,0:T(8,128)S(1)} %broadcast_in_dim.24), channel_id=1, replica_groups={{0,128,256,384},{8,136,264,392},{16,144,272,400},{24,152,280,408},{32,1..., dimensions={0} | all-to-all | bytes 114688 | tf_op jit(solution)/shard_map/all_to_all | solution.py:243
  74.7 10.3 %all_to_all.28 = f32[8,28,128]{2,1,0:T(8,128)S(1)} all-to-all(f32[8,28,128]{2,1,0:T(8,128)S(1)} %broadcast_in_dim.26), channel_id=1, replica_groups={{0,32,64,96,16,48,80,112},{8,40,72,104,24,56,88,120},{2,34,66,98,18,50,..., dimensions={0} | all-to-all | bytes 229376 | tf_op jit(solution)/shard_map/all_to_all | solution.py:243
  85.0 0.1 broadcast_in_dim.28
  85.1 16.1 %all_to_all.29 = f32[8,224,128]{2,1,0:T(8,128)S(1)} all-to-all(f32[8,224,128]{2,1,0:T(8,128)S(1)} %broadcast_in_dim.28), channel_id=1, replica_groups={{0,8,2,10,4,12,6,14},{16,24,18,26,20,28,22,30},{32,40,34,42,36,44,38,46..., dimensions={0} | all-to-all | bytes 1835008 | tf_op jit(solution)/shard_map/all_to_all | solution.py:243
  101.2 2.6 %collective-permute-start.1 = (f32[1792,128]{1,0:T(8,128)S(1)}, f32[1792,128]{1,0:T(8,128)S(1)}, u32[]{:S(2)}, u32[]{:S(2)}) collective-permute-start(f32[1792,128]{1,0:T(8,128)S(1)} %bitcast.8), channel_id=1, source_target_pairs={{0,1},{1,0},{2,3},{3,2},{4,5},{5,4},{6,7},{7,6},{8,9},{9,8},{10,11... | collective-permute-start | bytes 2752520 | tf_op jit(solution)/shard_map/ppermute | solution.py:281
  103.8 2.1 %collective-permute-done.1.other_ref = f32[1792,128]{1,0:T(8,128)S(1)} collective-permute-done((f32[1792,128]{1,0:T(8,128)S(1)}, f32[1792,128]{1,0:T(8,128)S(1)}, u32[]{:S(2)}, u32[]{:S(2)}) %collective-permute-start.1) | collective-permute-done | bytes 917536 | tf_op jit(solution)/shard_map/ppermute | solution.py:281
  105.9 28.4 %first_solve.1.step_ref = f32[8,896]{1,0:T(8,128)S(1)} custom-call(s32[1]{0:T(128)S(6)} %rem.18.core_ref, f32[1792,128]{1,0:T(8,128)S(1)} %bitcast.9, f32[1792,128]{1,0:T(8,128)S(1)} %collective-permute-done.1.other_ref), custom_call_target="tpu_custom_call" | custom-call | tf_op jit(solution)/shard_map/first_solve/pallas_call | solution.py:367
  134.3 1.4 %scen_steps.1 = (f32[896]{0:T(1024)}, f32[3,512]{1,0:T(4,128)}) custom-call(s32[1]{0:T(128)S(6)} %copy.9.live_ref, f32[8,896]{1,0:T(8,128)S(1)} %first_solve.1.step_ref, bf16[3,896,512]{2,1,0:T(8,128)(2,1)S(1)} %get-tuple-element.8.product_ref, f32[3,1,512]{2,1,0:T(1,128)S(1)} %get-tuple-element.9.reduced_ref), custom_call_target="tpu_custom_call" | custom-call | tf_op jit(solution)/shard_map/scen_steps/pallas_call | solution.py:457
  (7 shorter events, 0.1 us)
Async XLA Ops:
  9.2 10.9 %collective-permute-start = (f32[1792,128]{1,0:T(8,128)S(1)}, f32[1792,128]{1,0:T(8,128)S(1)}, u32[]{:S(2)}, u32[]{:S(2)}) collective-permute-start(f32[1792,128]{1,0:T(8,128)S(1)} %get-tuple-element.7), channel_id=1, source_target_pairs={{0,1},{1,0},{2,3},{3,2},{4,5},{5,4},{6,7},{7,6},{8,9},{9,8},{10,11... | collective-permute-start | bytes 2752520 | tf_op jit(solution)/shard_map/ppermute | solution.py:275
  101.2 4.7 %collective-permute-start.1 = (f32[1792,128]{1,0:T(8,128)S(1)}, f32[1792,128]{1,0:T(8,128)S(1)}, u32[]{:S(2)}, u32[]{:S(2)}) collective-permute-start(f32[1792,128]{1,0:T(8,128)S(1)} %bitcast.8), channel_id=1, source_target_pairs={{0,1},{1,0},{2,3},{3,2},{4,5},{5,4},{6,7},{7,6},{8,9},{9,8},{10,11... | collective-permute-start | bytes 2752520 | tf_op jit(solution)/shard_map/ppermute | solution.py:281
